TPU v7x, 256 devices: a whole 4x4x8 slice. The times are simulated.
256 devices in a mesh: row: 16 (over y, x), col: 16 (over z, core).
Axes of the slice: x: 4, y: 4, z: 8, core: 2. Of those that a mesh axis runs over, the one named last changes fastest.
Arguments:
- matrix: bfloat16 [24576, 24576], P('row', 'col'), may hold values from -6 to 6
- inverses: bfloat16 [2, 256, 256], replicated, may hold values from -0.09 to 0.1, as said below
Outputs:
- factored: bfloat16 [24576, 24576], P('row', 'col')
- panels: bfloat16 [24576, 512], P('row')
Inputs may be any that keep to these rules, and one draw needn't show every extreme that they name: `inverses`: each of the two matrices is lower triangular with a diagonal between 0.05 and 0.1.
All inputs are finite; a program needn't handle non-finite values.
Results may differ from a plain program's by a relative error of at most 0.0057.
Values may be sent and summed in bfloat16 or wider, within the bound.
No kernel may reach another device: no remote copies, remote signals or barrier semaphores. Data moves between devices by JAX's collectives and lax.ppermute only.
A program may use at most 128 MiB of HBM per device.

v0:
```python
import jax
import jax.numpy as jnp
from jax import lax
from jax.sharding import PartitionSpec as P


def from_root(value, axis, source):
    kept = jnp.where(lax.axis_index(axis) == source, value, 0).astype(value.dtype)
    return lax.psum(kept, axis)


def outer_term(left_rows, right_rows):
    return lax.dot_general(
        left_rows, right_rows, (((1,), (1,)), ((), ())), preferred_element_type=jnp.float32
    )


def shards(matrix, inverses):
    width = inverses.shape[1]
    rows_local = matrix.shape[0]
    row_count = lax.axis_size("row")
    col_count = lax.axis_size("col")
    row_rank = lax.axis_index("row")
    col_rank = lax.axis_index("col")
    blocks_row = rows_local // width
    blocks_col = matrix.shape[1] // width
    ratio_blocks = col_count // row_count
    global_rows = jnp.repeat(jnp.arange(blocks_row, dtype=jnp.int32) * row_count + row_rank, width)
    source_row = col_rank % row_count
    source_slot = col_rank // row_count

    def factor(panel, inverse, start_block, owner_col):
        product = jnp.dot(panel, inverse.T, preferred_element_type=jnp.float32)
        masked = jnp.where((global_rows >= start_block)[:, None], product, 0.0).astype(jnp.bfloat16)
        return from_root(masked, "col", owner_col)

    def columns_of(left_rows):
        gathered = lax.all_gather(left_rows, "row", axis=0, tiled=True)
        gathered = gathered.reshape(row_count, blocks_col, ratio_blocks, width, width)
        mine = lax.dynamic_index_in_dim(gathered, source_row, 0, keepdims=False)
        mine = lax.dynamic_index_in_dim(mine, source_slot, 1, keepdims=False)
        return mine.reshape(blocks_col * width, width)

    first_rows = factor(matrix[:, :width], inverses[0], 1, 0)
    first_cols = columns_of(first_rows)
    partial_value = matrix.astype(jnp.float32) - outer_term(first_rows, first_cols)
    head = partial_value[:, :width].astype(jnp.bfloat16)
    second_rows = factor(head, inverses[1], 2, 1)
    second_cols = columns_of(second_rows)
    factored = (partial_value - outer_term(second_rows, second_cols)).astype(jnp.bfloat16)
    return (factored, jnp.concatenate([first_rows, second_rows], axis=1))


def solution(mesh):
    return jax.shard_map(
        shards,
        mesh=mesh,
        in_specs=(P("row", "col"), P()),
        out_specs=(P("row", "col"), P("row", None)),
        check_vma=False,
    )
```

profile of v0, /device:TPU:1, one launch (start us, length us, event | category | flops | bytes accessed | tf_op | source)
XLA Modules:
  0.0 456.7 jit_solution(4977230878266750554)
XLA Ops:
  7.2 0.0 all-reduce.3.cloned.1.call-start
  7.2 0.1 broadcast_in_dim.30
  7.3 2.5 fusion.4
  9.8 0.0 all-reduce.3.cloned.1.call-update
  9.8 0.0 all-gather.3.cloned.1.call-start
  9.9 115.4 %all-reduce.3.cloned.1.call-done = bf16[1536,256]{1,0:T(8,128)(2,1)} async-done(((bf16[1536,256]{1,0:T(8,128)(2,1)}), bf16[1536,256]{1,0:T(8,128)(2,1)}) %all-reduce.3.cloned.1.call-update) | async-done | bytes 786448 | tf_op jit(solution)/shard_map/psum | solution.py:9
  125.2 0.0 all-gather.3.cloned.1.call-update
  125.3 0.0 all-reduce.5.cloned.1.call-start
  125.3 0.1 broadcast_in_dim.34
  125.4 98.0 %all-gather.3.cloned.1.call-done = bf16[24576,256]{1,0:T(8,128)(2,1)} async-done(((bf16[1536,256]{1,0:T(8,128)(2,1)}), bf16[24576,256]{1,0:T(8,128)(2,1)}) %all-gather.3.cloned.1.call-update) | async-done | bytes 12582928 | tf_op jit(solution)/shard_map/all_gather | solution.py:38
  223.4 1.2 constant_dynamic-slice_fusion.1
  224.6 0.0 copy-start.3
  224.6 4.0 convolution_subtract_fusion.1
  228.7 3.5 copy-done
  232.2 0.0 copy-done.3
  232.2 1.3 fusion.3
  233.5 0.0 all-reduce.5.cloned.1.call-update
  233.5 0.0 all-gather.5.cloned.1.call-start
  233.6 110.4 %all-reduce.5.cloned.1.call-done = bf16[1536,256]{1,0:T(8,128)(2,1)} async-done(((bf16[1536,256]{1,0:T(8,128)(2,1)}), bf16[1536,256]{1,0:T(8,128)(2,1)}) %all-reduce.5.cloned.1.call-update) | async-done | bytes 786448 | tf_op jit(solution)/shard_map/psum | solution.py:9
  343.9 0.0 all-gather.5.cloned.1.call-update
  344.0 2.5 pad_maximum_fusion
  346.4 95.2 %all-gather.5.cloned.1.call-done = bf16[24576,256]{1,0:T(8,128)(2,1)} async-done(((bf16[1536,256]{1,0:T(8,128)(2,1)}), bf16[24576,256]{1,0:T(8,128)(2,1)}) %all-gather.5.cloned.1.call-update) | async-done | bytes 12582928 | tf_op jit(solution)/shard_map/all_gather | solution.py:38
  441.6 1.2 constant_dynamic-slice_fusion
  442.8 7.3 %fusion = bf16[1536,1536]{1,0:T(8,128)(2,1)} fusion(f32[1536,1536]{1,0:T(8,128)} %copy-done, bf16[1536,256]{1,0:T(8,128)(2,1)S(1)} %copy-done.2, bf16[1536,256]{1,0:T(8,128)(2,1)S(1)} %bitcast.15), kind=kOutput, calls=%fused_computation.2 | convolution fusion | flops 1212678144 | bytes 15728640 | tf_op jit(solution)/shard_map/dot_general | solution.py:13
  (8 shorter events, 0.0 us)
Async XLA Ops:
  7.2 118.1 %all-reduce.3.cloned.1.call-start = ((), (), s32[]{:S(2)}) async-start(), calls=%async_computation | async-start | bytes 1572864 | tf_op jit(solution)/shard_map/psum | solution.py:9
  9.8 213.6 %all-gather.3.cloned.1.call-start = ((), (), s32[]{:S(2)}) async-start(), calls=%async_computation.1 | async-start | bytes 13369344 | tf_op jit(solution)/shard_map/all_gather | solution.py:38
  125.3 218.7 %all-reduce.5.cloned.1.call-start = ((), (), s32[]{:S(2)}) async-start(), calls=%async_computation.2 | async-start | bytes 1572864 | tf_op jit(solution)/shard_map/psum | solution.py:9
  224.6 7.6 %copy-start.3 = (bf16[2,256,256]{2,1,0:T(8,128)(2,1)S(1)}, bf16[2,256,256]{2,1,0:T(8,128)(2,1)}, u32[]{:S(2)}) copy-start(bf16[2,256,256]{2,1,0:T(8,128)(2,1)} %param.3) | copy-start | bytes 786436
  228.6 3.5 copy-start
  232.2 111.8 %copy-start.1 = (bf16[1536,256]{1,0:T(8,128)(2,1)S(1)}, bf16[1536,256]{1,0:T(8,128)(2,1)}, u32[]{:S(2)}) copy-start(bf16[1536,256]{1,0:T(8,128)(2,1)} %all-reduce.3.cloned.1.call-done) | copy-start | bytes 2359300
  233.5 208.1 %all-gather.5.cloned.1.call-start = ((), (), s32[]{:S(2)}) async-start(), calls=%async_computation.3 | async-start | bytes 13369344 | tf_op jit(solution)/shard_map/all_gather | solution.py:38
  343.9 98.9 %copy-start.2 = (bf16[1536,256]{1,0:T(8,128)(2,1)S(1)}, bf16[1536,256]{1,0:T(8,128)(2,1)}, u32[]{:S(2)}) copy-start(bf16[1536,256]{1,0:T(8,128)(2,1)} %all-reduce.5.cloned.1.call-done) | copy-start | bytes 2359300
Sparse Core Ops, SparseCore 0:
  10.9 114.2 all-reduce.2
  128.0 95.3 all-gather.2
  233.6 110.2 all-reduce.4
  346.2 95.3 all-gather.4
where the time goes:
time: 457 us
  waiting for transfers between devices  419 us (92%)
  matrix products  15.1 us (3%)
  between operations  13.8 us (3%)
  local copies, waits for them, and re-layouts  6.09 us (1%)
    psum x2, waiting for transfers between devices, from_root(): return lax.psum(kept, axis)  226 us
    all_gather x2, waiting for transfers between devices, columns_of(): gathered = lax.all_gather(left_rows, 'row', axis=0, tiled=True)  193 us
    dot_general x2, matrix products, outer_term(): lax.dot_general(left_rows, right_rows, (((1,), (1,)), ((), ())), preferre...  11.3 us
  transfers between devices with their start and end apart: 4, of which 4 were waited for; matrix products, arithmetic and copies ran while one was open for 1% of the time, Pallas kernels for 0%

commit v1 on v0

--- a/solution.py
+++ b/solution.py
@@ -35,7 +35,11 @@
         return from_root(masked, "col", owner_col)
 
     def columns_of(left_rows):
-        gathered = lax.all_gather(left_rows, "row", axis=0, tiled=True)
+        peers = lax.axis_size("row")
+        repeats = [peers if d == 0 else 1 for d in range(left_rows.ndim)]
+        gathered = lax.all_to_all(
+            jnp.tile(left_rows, repeats), "row", split_axis=0, concat_axis=0, tiled=True
+        )
         gathered = gathered.reshape(row_count, blocks_col, ratio_blocks, width, width)
         mine = lax.dynamic_index_in_dim(gathered, source_row, 0, keepdims=False)
         mine = lax.dynamic_index_in_dim(mine, source_slot, 1, keepdims=False)

time: 457 us -> 665 us (1.46)
  waiting for transfers between devices: 419 us -> 596 us
  local copies, waits for them, and re-layouts: 6.09 us -> 19.8 us
  starting transfers between devices: 0.16 us -> 13.5 us
    all_to_all x0 -> x2, waiting for transfers between devices: none -> 369 us  [columns_of(): lax.all_to_all(jnp.tile(left_rows, repeats), 'row', split_axis=0, concat_...]
    all_gather x2 -> x0, waiting for transfers between devices: 193 us -> none  [columns_of(): gathered = lax.all_gather(left_rows, 'row', axis=0, tiled=True)]
    another operation x0 -> x2, local copies, waits for them, and re-layouts: none -> 13.6 us  [columns_of(): jnp.tile(left_rows, repeats)]
    all_to_all x0 -> x2, starting transfers between devices: none -> 13.4 us  [columns_of(): lax.all_to_all(jnp.tile(left_rows, repeats), 'row', split_axis=0, concat_...]
  transfers between devices with their start and end apart: 4 -> 4, of which waited for: 4 -> 4; matrix products, arithmetic and copies ran while one was open for 1% -> 0% of each run, Pallas kernels for 0% -> 0%
where the time goes in v1:
time: 665 us; the launch traced here: 660 us
  waiting for transfers between devices  596 us (90%)
  local copies, waits for them, and re-layouts  19.8 us (3%)
  matrix products  14.9 us (2%)
  between operations  14.1 us (2%)
  starting transfers between devices  13.5 us (2%)
    all_to_all x2, waiting for transfers between devices, columns_of(): lax.all_to_all(jnp.tile(left_rows, repeats), 'row', split_axis=0, concat_...  369 us
    psum x2, waiting for transfers between devices, from_root(): return lax.psum(kept, axis)  227 us
    another operation x2, local copies, waits for them, and re-layouts, columns_of(): jnp.tile(left_rows, repeats)  13.6 us
    all_to_all x2, starting transfers between devices, columns_of(): lax.all_to_all(jnp.tile(left_rows, repeats), 'row', split_axis=0, concat_...  13.4 us
  transfers between devices with their start and end apart: 4, of which 4 were waited for; matrix products, arithmetic and copies ran while one was open for 0% of the time, Pallas kernels for 0%

profile of v1, /device:TPU:1, one launch (start us, length us, event | category | flops | bytes accessed | tf_op | source)
XLA Modules:
  0.0 659.8 jit_solution(13167815841436633145)
XLA Ops:
  7.2 0.0 all-reduce.3.cloned.1.call-start
  7.2 0.1 broadcast_in_dim.30
  7.3 2.5 fusion.4
  9.8 0.0 all-reduce.3.cloned.1.call-update
  9.8 115.4 %all-reduce.3.cloned.1.call-done = bf16[1536,256]{1,0:T(8,128)(2,1)} async-done(((bf16[1536,256]{1,0:T(8,128)(2,1)}), bf16[1536,256]{1,0:T(8,128)(2,1)}) %all-reduce.3.cloned.1.call-update) | async-done | bytes 786448 | tf_op jit(solution)/shard_map/psum | solution.py:9
  125.2 6.8 %tile.4 = bf16[16,1536,256]{2,1,0:T(8,128)(2,1)} broadcast(bf16[1536,256]{1,0:T(8,128)(2,1)} %all-reduce.3.cloned.1.call-done), dimensions={1,2} | broadcast | bytes 13369344 | tf_op jit(solution)/shard_map/tile | solution.py:41
  132.1 6.7 %all-to-all-start = ((bf16[16,1536,256]{2,1,0:T(8,128)(2,1)}), bf16[16,1536,256]{2,1,0:T(8,128)(2,1)}, u32[]{:S(2)}, u32[]{:S(2)}) async-start(bf16[16,1536,256]{2,1,0:T(8,128)(2,1)} %tile.4), calls=%async_computation | async-start | bytes 25165824 | tf_op jit(solution)/shard_map/all_to_all | solution.py:40
  138.8 0.0 all-reduce.5.cloned.1.call-start
  138.8 0.1 broadcast_in_dim.34
  138.9 185.2 %all-to-all-done = bf16[16,1536,256]{2,1,0:T(8,128)(2,1)} async-done(((bf16[16,1536,256]{2,1,0:T(8,128)(2,1)}), bf16[16,1536,256]{2,1,0:T(8,128)(2,1)}, u32[]{:S(2)}, u32[]{:S(2)}) %all-to-all-start) | async-done | bytes 12582944 | tf_op jit(solution)/shard_map/all_to_all | solution.py:40
  324.1 1.2 constant_dynamic-slice_fusion.1
  325.3 0.0 copy-done.1
  325.3 0.0 copy-start.3
  325.3 3.8 convolution_subtract_fusion.1
  329.1 3.6 copy-done
  332.7 1.3 fusion.3
  334.0 0.0 all-reduce.5.cloned.1.call-update
  334.0 111.6 %all-reduce.5.cloned.1.call-done = bf16[1536,256]{1,0:T(8,128)(2,1)} async-done(((bf16[1536,256]{1,0:T(8,128)(2,1)}), bf16[1536,256]{1,0:T(8,128)(2,1)}) %all-reduce.5.cloned.1.call-update) | async-done | bytes 786448 | tf_op jit(solution)/shard_map/psum | solution.py:9
  445.6 6.8 %tile.5 = bf16[16,1536,256]{2,1,0:T(8,128)(2,1)} broadcast(bf16[1536,256]{1,0:T(8,128)(2,1)} %all-reduce.5.cloned.1.call-done), dimensions={1,2} | broadcast | bytes 13369344 | tf_op jit(solution)/shard_map/tile | solution.py:41
  452.4 6.7 %all-to-all-start.1 = ((bf16[16,1536,256]{2,1,0:T(8,128)(2,1)}), bf16[16,1536,256]{2,1,0:T(8,128)(2,1)}, u32[]{:S(2)}, u32[]{:S(2)}) async-start(bf16[16,1536,256]{2,1,0:T(8,128)(2,1)} %tile.5), calls=%async_computation.1 | async-start | bytes 25165824 | tf_op jit(solution)/shard_map/all_to_all | solution.py:40
  459.1 1.3 pad_maximum_fusion
  460.4 184.0 %all-to-all-done.1 = bf16[16,1536,256]{2,1,0:T(8,128)(2,1)} async-done(((bf16[16,1536,256]{2,1,0:T(8,128)(2,1)}), bf16[16,1536,256]{2,1,0:T(8,128)(2,1)}, u32[]{:S(2)}, u32[]{:S(2)}) %all-to-all-start.1) | async-done | bytes 12582944 | tf_op jit(solution)/shard_map/all_to_all | solution.py:40
  644.4 1.2 constant_dynamic-slice_fusion
  645.6 7.3 %fusion = bf16[1536,1536]{1,0:T(8,128)(2,1)} fusion(f32[1536,1536]{1,0:T(8,128)} %copy-done, bf16[1536,256]{1,0:T(8,128)(2,1)S(1)} %copy-done.2, bf16[1536,256]{1,0:T(8,128)(2,1)S(1)} %bitcast.15), kind=kOutput, calls=%fused_computation.2 | convolution fusion | flops 1212678144 | bytes 15728640 | tf_op jit(solution)/shard_map/dot_general | solution.py:13
  (8 shorter events, 0.0 us)
Async XLA Ops:
  7.2 118.1 %all-reduce.3.cloned.1.call-start = ((), (), s32[]{:S(2)}) async-start(), calls=%async_computation.2 | async-start | bytes 1572864 | tf_op jit(solution)/shard_map/psum | solution.py:9
  132.1 193.2 %copy-start.1 = (bf16[1536,256]{1,0:T(8,128)(2,1)S(1)}, bf16[1536,256]{1,0:T(8,128)(2,1)}, u32[]{:S(2)}) copy-start(bf16[1536,256]{1,0:T(8,128)(2,1)} %all-reduce.3.cloned.1.call-done) | copy-start | bytes 2359300
  132.1 192.0 %all-to-all-start = ((bf16[16,1536,256]{2,1,0:T(8,128)(2,1)}), bf16[16,1536,256]{2,1,0:T(8,128)(2,1)}, u32[]{:S(2)}, u32[]{:S(2)}) async-start(bf16[16,1536,256]{2,1,0:T(8,128)(2,1)} %tile.4), calls=%async_computation | async-start | bytes 25165824 | tf_op jit(solution)/shard_map/all_to_all | solution.py:40
  138.8 306.8 %all-reduce.5.cloned.1.call-start = ((), (), s32[]{:S(2)}) async-start(), calls=%async_computation.3 | async-start | bytes 1572864 | tf_op jit(solution)/shard_map/psum | solution.py:9
  325.3 7.4 %copy-start.3 = (bf16[2,256,256]{2,1,0:T(8,128)(2,1)S(1)}, bf16[2,256,256]{2,1,0:T(8,128)(2,1)}, u32[]{:S(2)}) copy-start(bf16[2,256,256]{2,1,0:T(8,128)(2,1)} %param.3) | copy-start | bytes 786436
  329.1 3.6 copy-start
  452.4 6.7 %copy-start.2 = (bf16[1536,256]{1,0:T(8,128)(2,1)S(1)}, bf16[1536,256]{1,0:T(8,128)(2,1)}, u32[]{:S(2)}) copy-start(bf16[1536,256]{1,0:T(8,128)(2,1)} %all-reduce.5.cloned.1.call-done) | copy-start | bytes 2359300
  452.4 192.0 %all-to-all-start.1 = ((bf16[16,1536,256]{2,1,0:T(8,128)(2,1)}), bf16[16,1536,256]{2,1,0:T(8,128)(2,1)}, u32[]{:S(2)}, u32[]{:S(2)}) async-start(bf16[16,1536,256]{2,1,0:T(8,128)(2,1)} %tile.5), calls=%async_computation.1 | async-start | bytes 25165824 | tf_op jit(solution)/shard_map/all_to_all | solution.py:40
Sparse Core Ops, SparseCore 0:
  10.9 114.2 all-reduce.2
  334.1 111.4 all-reduce.4
